TPU v7x, 32 devices: a whole 2x2x4 slice. The times are simulated.
32 devices in a mesh: groups: 2 (over x), tile: 16 (over z, y, core).
Axes of the slice: x: 2, y: 2, z: 4, core: 2. Of those that a mesh axis runs over, the one named last changes fastest.
Arguments:
- strain: bfloat16 [12288, 2, 4096], P(('groups', 'tile')), parts along dimension 0, may hold values from -6 to 6
- tile_pairs: int32 [96, 2], P(('groups', 'tile')), parts along dimension 0, may hold values from 0 to 47, as said below
- tile_count: int32 [32], P(('groups', 'tile')), parts along dimension 0, may hold values from 2 to 3, as said below
Outputs:
- correlations: bfloat16 [96, 128, 8192], P(('groups', 'tile')), parts along dimension 0
There are 2 independent parts, one for each index of `groups`. A program takes and returns all parts, laid end to end along the dimension named above; each array names one. Nothing has to cross between parts.
Inputs may be any that keep to these rules, and one draw needn't show every extreme that they name: `tile_pairs`: row k holds row block k and a column block from k to k + 6; where k mod 3 is 0, the column block is k + 6, where it is 1, k + 3, or the last block where that lies beyond it. `tile_count`: some device has all 3 tiles live in every draw.
All inputs are finite; a program needn't handle non-finite values.
Results may differ from a plain program's by a relative error of at most 0.0075.
Values may be sent and summed in bfloat16 or wider, within the bound.
No kernel may reach another device: no remote copies, remote signals or barrier semaphores. Data moves between devices by JAX's collectives and lax.ppermute only.
A program may use at most 128 MiB of HBM per device.

v0:
```python
import functools
import math

import jax
import jax.numpy as jnp
import numpy as np
from jax import lax
from jax.experimental import pallas as pl
from jax.experimental.pallas import tpu as pltpu
from jax.sharding import PartitionSpec as P

CH = 128
WIN = 4096
BAND = 256
BIN0 = 60
SMOOTH = 64
LAGS = 64
ROWS = 16
PITCH = 72
BF16 = jnp.bfloat16
F32 = jnp.float32


def bin_order():
    return np.concatenate([np.arange(0, BAND, 2), np.arange(1, BAND, 2)])


def dft_tables():
    times = np.arange(WIN // 2, dtype=np.int64)[:, None]
    tables = []
    for parity in range(2):
        freqs = BIN0 + np.arange(parity, BAND, 2, dtype=np.int64)[None, :]
        angle = (times * freqs % WIN) * (2.0 * math.pi / WIN)
        tables.append(np.concatenate([np.cos(angle), -np.sin(angle)], 1))
    group = bin_order() // SMOOTH
    tables.append((group[:, None] == group[None, :]) / SMOOTH)
    return np.concatenate(tables, 0).astype(BF16)


def phase_tables(coarse, scale):
    fine = LAGS // coarse
    freqs = (BIN0 + bin_order())[None, :]
    lags_a = fine * np.arange(1, coarse // 2 + 1)[:, None]
    lags_b = np.arange(fine)[:, None]
    step = 2.0 * math.pi / WIN
    a = np.concatenate([np.cos(lags_a * freqs * step), np.sin(lags_a * freqs * step)], 1) * scale
    b = np.concatenate([np.cos(lags_b * freqs * step), np.sin(lags_b * freqs * step)], 1)
    return a.astype(np.float32), b.astype(np.float32)


def spectra_kernel(blocks, wins, x_hbm, tab_hbm, w0_ref, w1_ref, all_ref, x, tab, rows, left, x_sem, t_sem):
    part = CH // 2
    half = WIN // 2
    per = WIN // 128 * wins

    def x_copy(n):
        channels = pl.ds(n * part, part)
        return pltpu.make_async_copy(x_hbm.at[channels], x.at[channels], x_sem.at[n])

    t_copy = pltpu.make_async_copy(tab_hbm, tab, t_sem)
    x_copy(0).start()
    x_copy(1).start()
    t_copy.start()
    for n in range(2, 2 * blocks):
        x_copy(n).start()

    def fold(b, side):
        first = side * part
        for c in range(first, first + part):
            rows[c * PITCH : c * PITCH + per, :] = x[b * CH + c].astype(F32)
        for t in range(half // 128):
            for w in range(wins):
                row = first * PITCH + t * wins + w
                head = rows[pl.ds(row, part, stride=PITCH), :]
                tail = rows[pl.ds(row + per // 2, part, stride=PITCH), :]
                place = (slice(w * CH + first, w * CH + first + part), slice(t * 128, (t + 1) * 128))
                left[2 * b, place[0], place[1]] = (head + tail).astype(BF16)
                left[2 * b + 1, place[0], place[1]] = (head - tail).astype(BF16)

    def finish(b):
        spec = [
            jnp.dot(
                left[2 * b + sign],
                tab[sign * half : (sign + 1) * half, :],
                preferred_element_type=F32,
            )
            for sign in range(2)
        ]
        mean = tab[2 * half :, :]
        energy = [s[:, :128] * s[:, :128] + s[:, 128:] * s[:, 128:] for s in spec]
        energy = jnp.concatenate(energy, 1)
        high = energy.astype(BF16)
        low = (energy - high.astype(F32)).astype(BF16)
        power = jnp.dot(high, mean, preferred_element_type=F32)
        power += jnp.dot(low, mean, preferred_element_type=F32)
        factor = lax.rsqrt(power + 1e-06)
        for w in range(wins):
            r = slice(w * CH, (w + 1) * CH)
            for q in range(4):
                sign, side = q % 2, q // 2
                value = spec[sign][r, side * 128 : (side + 1) * 128]
                value = (value * factor[r, sign * 128 : (sign + 1) * 128]).astype(BF16)
                column = (w * 4 + q) * 128
                all_ref[b, :, column : column + 128] = value
                if b < 2:
                    (w0_ref, w1_ref)[b][:, column : column + 128] = value

    x_copy(0).wait()
    fold(0, 0)
    x_copy(1).wait()
    fold(0, 1)
    t_copy.wait()
    for b in range(1, blocks):
        x_copy(2 * b).wait()
        x_copy(2 * b + 1).wait()
        finish(b - 1)
        fold(b, 0)
        fold(b, 1)
    finish(blocks - 1)


def spectra(view, table, blocks, wins):
    depth = wins * 2 * BAND
    shapes = [(CH, depth), (CH, depth), (blocks, CH, depth)]
    return pl.pallas_call(
        functools.partial(spectra_kernel, blocks, wins),
        out_shape=[jax.ShapeDtypeStruct(shape, BF16) for shape in shapes],
        in_specs=[pl.BlockSpec(memory_space=pl.ANY)] * 2,
        out_specs=[pl.BlockSpec(memory_space=pltpu.VMEM)] * len(shapes),
        scratch_shapes=[
            pltpu.VMEM(view.shape, BF16),
            pltpu.VMEM(table.shape, BF16),
            pltpu.VMEM((CH * PITCH, 128), F32),
            pltpu.VMEM((2 * blocks, CH * wins, WIN // 2), BF16),
            pltpu.SemaphoreType.DMA((2 * blocks,)),
            pltpu.SemaphoreType.DMA,
        ],
        compiler_params=pltpu.CompilerParams(vmem_limit_bytes=52 * 2**20),
        cost_estimate=pl.CostEstimate(
            flops=2 * blocks * CH * wins * WIN * BAND,
            bytes_accessed=2 * blocks * CH * wins * WIN + 2 * WIN * BAND,
            transcendentals=0,
        ),
        name="spectra",
    )(view, table)


def chosen(want, everything, other):
    blocks = everything.shape[0]
    me = lax.axis_index("tile")
    index = want - me * blocks
    own = lax.dynamic_index_in_dim(everything, jnp.clip(index, 0, blocks - 1), 0, keepdims=False)
    beside = lax.dynamic_index_in_dim(
        other, jnp.clip(index + blocks, 0, blocks - 1), 0, keepdims=False
    )
    return jnp.where(jnp.logical_or(index >= 0, me % 2 == 0), own, beside)


def corr_kernel(slots, blocks, scale, coarse, *refs):
    fine = LAGS // coarse
    js = 256 // fine
    chunks = CH // js
    count = len(slots)
    pairs_ref, count_ref, atab_ref, btab_ref, all_ref, other_ref = refs[:6]
    fars = refs[6 : 6 + count]
    row_refs = refs[6 + count : 6 + 2 * count]
    out_hbm, raw, col, acoef, b0, b1, p0, p1, obuf, in_sem, out_sem = refs[-11:]
    me = lax.axis_index("tile")
    even = me % 2 == 0

    def out_copy(n, c):
        columns = pl.ds(c * js * LAGS, js * LAGS)
        return pltpu.make_async_copy(
            obuf.at[n, :, columns], out_hbm.at[slots[n], :, columns], out_sem.at[n, c]
        )

    def fetch(n):
        index = pairs_ref[slots[n], 1] - me * blocks
        own = index < blocks
        beside = jnp.logical_and(index >= blocks, jnp.logical_and(even, index < 2 * blocks))
        remote = jnp.logical_not(jnp.logical_or(own, beside))

        @pl.when(own)
        def _():
            source = all_ref.at[jnp.clip(index, 0, blocks - 1)]
            pltpu.make_async_copy(source, raw.at[n], in_sem.at[n]).start()

        @pl.when(beside)
        def _():
            source = other_ref.at[jnp.clip(index - blocks, 0, blocks - 1)]
            pltpu.make_async_copy(source, raw.at[n], in_sem.at[n]).start()

        @pl.when(remote)
        def _():
            pltpu.make_async_copy(fars[n], raw.at[n], in_sem.at[n]).start()

    def prepare(n):
        live = jnp.where(count_ref[0] > slots[n], 1.0, 0.0).astype(F32)
        for w in range(2):
            for p in range(2):
                re_cols = slice((w * 4 + p) * 128, (w * 4 + p + 1) * 128)
                im_cols = slice((w * 4 + 2 + p) * 128, (w * 4 + 3 + p) * 128)
                re = row_refs[n][0, :, re_cols].astype(F32)
                im = row_refs[n][0, :, im_cols].astype(F32)

                def put(a, re_value, im_value):
                    rows = slice(a * CH, (a + 1) * CH)
                    acoef[n, rows, re_cols] = re_value.astype(BF16)
                    acoef[n, rows, im_cols] = im_value.astype(BF16)

                middle = coarse // 2
                put(middle, re * (scale * live), im * (scale * live))
                for k in range(1, middle + 1):
                    cos = atab_ref[k - 1 : k, p * 128 : (p + 1) * 128] * live
                    sin = atab_ref[k - 1 : k, (2 + p) * 128 : (3 + p) * 128] * live
                    rc, ic, rs, ims = re * cos, im * cos, re * sin, im * sin
                    put(middle - k, rc + ims, ic - rs)
                    if k < middle:
                        put(middle + k, rc - ims, ic + rs)

    def build(n, c, b):
        for w in range(2):
            for p in range(2):
                re_q, im_q = w * 4 + p, w * 4 + 2 + p
                cos = btab_ref[:, p * 128 : (p + 1) * 128]
                sin = btab_ref[:, (2 + p) * 128 : (3 + p) * 128]
                step = max(ROWS // fine, 1)
                for place in range(0, js, step):
                    res, ims = [], []
                    for pos in range(place, place + step):
                        v, inner = divmod(pos, 2 * coarse)
                        jj, q = divmod(inner, coarse)
                        j = c * js + v * 2 * coarse + 2 * q + jj
                        re = col[n, re_q, pl.ds(j, 8, stride=0), :]
                        im = col[n, im_q, pl.ds(j, 8, stride=0), :]
                        re = jnp.concatenate([re] * (fine // 8), 0)
                        im = jnp.concatenate([im] * (fine // 8), 0)
                        res.append(re * cos + im * sin)
                        ims.append(im * cos - re * sin)
                    rows = slice(place * fine, (place + step) * fine)
                    b[rows, re_q * 128 : (re_q + 1) * 128] = jnp.concatenate(res, 0).astype(BF16)
                    b[rows, im_q * 128 : (im_q + 1) * 128] = jnp.concatenate(ims, 0).astype(BF16)

    def multiply(n, b, p):
        p[...] = lax.dot_general(
            acoef[n], b[...], (((1,), (1,)), ((), ())), preferred_element_type=F32
        )

    lane = lax.broadcasted_iota(jnp.int32, (CH, 128), 1)

    def arrange(n, c, prod):
        for v in range(2):
            x = [prod[a * CH : (a + 1) * CH, v * 128 : (v + 1) * 128] for a in range(coarse)]
            bit = 1
            while bit < coarse:
                upper = (lane // fine) & bit != 0
                for a in range(coarse):
                    if a & bit == 0:
                        lo, hi = x[a], x[a | bit]
                        x[a] = jnp.where(upper, pltpu.roll(hi, fine * bit, 1), lo)
                        x[a | bit] = jnp.where(upper, hi, pltpu.roll(lo, 128 - fine * bit, 1))
                bit *= 2
            for q in range(coarse):
                column = c * js * LAGS + (v * coarse + q) * 128
                obuf[n, :, column : column + 128] = x[q].astype(BF16)
        out_copy(n, c).start()

    def run():
        for n in range(count):
            fetch(n)
        prepare(0)
        for n in range(count):
            pltpu.make_async_copy(fars[n], raw.at[n], in_sem.at[n]).wait()
        bs, ps = (b0, b1), (p0, p1)
        steps = [(n, c) for n in range(count) for c in range(chunks)]

        def ready(k):
            n, c = steps[k]
            if c == 0:
                if n > 0:
                    prepare(n)
                for q in range(8):
                    col[n, q] = raw[n, :, q * 128 : (q + 1) * 128].astype(F32)
            build(n, c, bs[k % 2])

        ready(0)
        for k, (n, c) in enumerate(steps):
            multiply(n, bs[k % 2], ps[k % 2])
            if k > 0:
                arrange(*steps[k - 1], ps[(k - 1) % 2])
            if k + 1 < len(steps):
                ready(k + 1)
        arrange(*steps[-1], ps[(len(steps) - 1) % 2])

    if count == 1:
        live = count_ref[0] > slots[0]
        pl.when(live)(run)

        @pl.when(jnp.logical_not(live))
        def _():
            obuf[...] = jnp.zeros_like(obuf)
            for c in range(chunks):
                out_copy(0, c).start()
    else:
        run()
    for n in range(count):
        for c in range(chunks):
            out_copy(n, c).wait()


def corr_tiles(slots, scale, coarse, pairs, tile_count, everything, other, fars, buffer):
    fine = LAGS // coarse
    tables = [jnp.asarray(t) for t in phase_tables(coarse, scale)]
    js = 256 // fine
    chunks = CH // js
    count = len(slots)
    blocks, _, depth = everything.shape
    in_specs = [
        pl.BlockSpec(memory_space=pltpu.SMEM),
        pl.BlockSpec(memory_space=pltpu.SMEM),
        pl.BlockSpec(memory_space=pltpu.VMEM),
        pl.BlockSpec(memory_space=pltpu.VMEM),
    ] + [pl.BlockSpec(memory_space=pl.ANY)] * (2 + count)
    in_specs += [pl.BlockSpec((1, CH, depth), lambda i, s=s: (s, 0, 0)) for s in slots]
    operands = [pairs, tile_count, *tables, everything, other, *fars] + [everything] * count
    aliases = {}
    if buffer is not None:
        aliases = {len(operands): 0}
        operands.append(buffer)
        in_specs.append(pl.BlockSpec(memory_space=pl.ANY))
    return pl.pallas_call(
        functools.partial(corr_kernel, slots, blocks, scale, coarse),
        grid=(1,),
        out_shape=jax.ShapeDtypeStruct((blocks, CH, CH * LAGS), BF16),
        in_specs=in_specs,
        out_specs=pl.BlockSpec(memory_space=pl.ANY),
        scratch_shapes=[
            pltpu.VMEM((count, CH, depth), BF16),
            pltpu.VMEM((count, 8, CH, 128), F32),
            pltpu.VMEM((count, coarse * CH, depth), BF16),
            pltpu.VMEM((js * fine, depth), BF16),
            pltpu.VMEM((js * fine, depth), BF16),
            pltpu.VMEM((coarse * CH, js * fine), F32),
            pltpu.VMEM((coarse * CH, js * fine), F32),
            pltpu.VMEM((count, CH, CH * LAGS), BF16),
            pltpu.SemaphoreType.DMA((count,)),
            pltpu.SemaphoreType.DMA((count, chunks)),
        ],
        input_output_aliases=aliases,
        compiler_params=pltpu.CompilerParams(vmem_limit_bytes=32 * 2**20),
        cost_estimate=pl.CostEstimate(
            flops=4 * count * CH * CH * LAGS * depth,
            bytes_accessed=2 * count * CH * CH * LAGS,
            transcendentals=0,
        ),
        name="lags_" + "_".join(str(s) for s in slots),
    )(*operands)


def body(strain, tile_pairs, tile_count):
    blocks = strain.shape[0] // CH
    wins = strain.shape[1]
    size = lax.axis_size("tile")
    depth = wins * 2 * BAND
    scale = 1.0 / math.sqrt(wins * BAND)
    table = jnp.asarray(dft_tables())
    ahead2 = [(i, i - 2) for i in range(2, size)]
    behind2 = [(i, i + 2) for i in range(size - 2)]
    across = [(i, i - 1) for i in range(2, size, 2)]
    swap = [(i, i ^ 1) for i in range(size)]

    view = strain.reshape(blocks * CH, wins, WIN // 128, 128).transpose(0, 2, 1, 3)
    view = view.reshape(blocks * CH, WIN // 128 * wins, 128)
    want = lax.ppermute(tile_pairs, "tile", behind2)[blocks - 1, 1]
    w0, w1, everything = spectra(view, table, blocks, wins)
    far0 = lax.ppermute(w0, "tile", ahead2)
    near1 = lax.ppermute(w1, "tile", across)
    other = lax.ppermute(everything, "tile", swap)
    far2 = lax.ppermute(chosen(want, everything, other), "tile", ahead2)
    shared = (scale, 4, tile_pairs, tile_count, everything, other)
    out = corr_tiles((0, 1), *shared, (far0, near1), None)
    return corr_tiles((2,), *shared, (far2,), out)


def solution(mesh):
    in_specs = (
        P(("groups", "tile"), None, None),
        P(("groups", "tile"), None),
        P(("groups", "tile")),
    )
    out_specs = P(("groups", "tile"), None, None)
    return jax.shard_map(body, mesh=mesh, in_specs=in_specs, out_specs=out_specs, check_vma=False)
```

profile of v0, /device:TPU:28, one launch (start us, length us, event | category | flops | bytes accessed | tf_op | source)
XLA Modules:
  0.0 39.0 jit_solution(9160502998382674426)
XLA Ops:
  0.0 0.0 copy-start
  0.0 0.0 copy-start.1
  0.0 0.0 copy-start.2
  0.0 8.0 %spectra.1 = (bf16[128,1024]{1,0:T(8,128)(2,1)S(1)}, bf16[128,1024]{1,0:T(8,128)(2,1)S(1)}, bf16[3,128,1024]{2,1,0:T(8,128)(2,1)S(1)}) custom-call(bf16[384,64,128]{2,1,0:T(8,128)(2,1)} %bitcast.8, bf16[4352,256]{1,0:T(8,128)(2,1)} %constant.34.clone.tab_hbm), custom_call_target="tpu_custom_call" | custom-call | flops 1610612736 | bytes 8388608 | tf_op jit(solution)/shard_map/spectra/pallas_call | solution.py:125
  8.0 0.1 collective-permute-start
  8.1 2.4 %collective-permute-start.3 = (bf16[128,1024]{1,0:T(8,128)(2,1)S(1)}, bf16[128,1024]{1,0:T(8,128)(2,1)S(1)}, u32[]{:S(2)}, u32[]{:S(2)}) collective-permute-start(bf16[128,1024]{1,0:T(8,128)(2,1)S(1)} %get-tuple-element.9), channel_id=1, source_target_pairs={{2,0},{3,1},{4,2},{5,3},{6,4},{7,5},{8,6},{9,7},{10,8},{11,9},{12,... | collective-permute-start | bytes 786440 | tf_op jit(solution)/shard_map/ppermute | solution.py:376
  10.6 3.1 %collective-permute-start.4 = (bf16[128,1024]{1,0:T(8,128)(2,1)S(1)}, bf16[128,1024]{1,0:T(8,128)(2,1)S(1)}, u32[]{:S(2)}, u32[]{:S(2)}) collective-permute-start(bf16[128,1024]{1,0:T(8,128)(2,1)S(1)} %get-tuple-element.10), channel_id=1, source_target_pairs={{2,1},{4,3},{6,5},{8,7},{10,9},{12,11},{14,13},{18,17},{20,19},{22... | collective-permute-start | bytes 786440 | tf_op jit(solution)/shard_map/ppermute | solution.py:377
  13.7 0.0 copy-done.2
  13.7 1.3 %collective-permute-start.1 = (s32[3,2]{0,1:T(2,128)S(1)}, s32[3,2]{0,1:T(2,128)S(1)}, u32[]{:S(2)}, u32[]{:S(2)}) collective-permute-start(s32[3,2]{0,1:T(2,128)S(1)} %copy-done.2), channel_id=1, source_target_pairs={{0,2},{1,3},{2,4},{3,5},{4,6},{5,7},{6,8},{7,9},{8,10},{9,11},{10,... | collective-permute-start | bytes 80 | tf_op jit(solution)/shard_map/ppermute | solution.py:374
  15.0 0.1 copy.12.refs_0_
  15.7 3.4 %collective-permute-done.1 = s32[3,2]{0,1:T(2,128)S(1)} collective-permute-done((s32[3,2]{0,1:T(2,128)S(1)}, s32[3,2]{0,1:T(2,128)S(1)}, u32[]{:S(2)}, u32[]{:S(2)}) %collective-permute-start.1) | collective-permute-done | bytes 56 | tf_op jit(solution)/shard_map/ppermute | solution.py:374
  19.2 0.6 %slice.3 = s32[1,1]{0,1:T(1,128)} slice(s32[3,2]{0,1:T(2,128)S(1)} %collective-permute-done.1), slice={[2:3], [1:2]} | slice | bytes 8 | tf_op jit(solution)/shard_map/slice | solution.py:374
  20.4 0.0 collective-permute-done.refs_5_
  20.5 3.3 %collective-permute-start.2 = (bf16[128,1024]{1,0:T(8,128)(2,1)S(1)}, bf16[128,1024]{1,0:T(8,128)(2,1)S(1)}, u32[]{:S(2)}, u32[]{:S(2)}) collective-permute-start(bf16[128,1024]{1,0:T(8,128)(2,1)S(1)} %select_bitcast_fusion), channel_id=1, source_target_pairs={{2,0},{3,1},{4,2},{5,3},{6,4},{7,5},{8,6},{9,7},{10,8},{11,9},{12,... | collective-permute-start | bytes 786440 | tf_op jit(solution)/shard_map/ppermute | solution.py:379
  23.8 0.0 collective-permute-done.3.refs_6_
  23.8 0.0 collective-permute-done.4.refs_7_
  23.8 0.0 copy-done
  23.8 0.0 copy-done.1
  23.8 9.6 %lags_0_1.1.refs_8_ = bf16[3,128,8192]{2,1,0:T(8,128)(2,1)} custom-call(s32[3,2]{1,0:T(4,128)S(1)} %copy.12.refs_0_, s32[1]{0:T(128)S(6)} %copy.14.refs_1_, f32[2,512]{1,0:T(2,128)S(1)} %copy-done.1, f32[16,512]{1,0:T(8,128)S(1)} %copy-done, bf16[3,128,1024]{2,1,0:T(8,128)(2,1)S(1)} %get-tuple-element.8.refs_4_.refs_8_.refs_9_.refs_7_, ...), custom_call_target="tpu_custom_call" | custom-call | flops 8589934592 | bytes 4194304 | tf_op jit(solution)/shard_map/lags_0_1/pallas_call | solution.py:331
  33.5 0.0 collective-permute-done.2.refs_6_
  33.5 5.4 %lags_2.1 = bf16[3,128,8192]{2,1,0:T(8,128)(2,1)} custom-call(s32[3,2]{1,0:T(4,128)S(1)} %copy.12.refs_0_, s32[1]{0:T(128)S(6)} %copy.14.refs_1_, f32[2,512]{1,0:T(2,128)S(1)} %copy-done.1, f32[16,512]{1,0:T(8,128)S(1)} %copy-done, bf16[3,128,1024]{2,1,0:T(8,128)(2,1)S(1)} %get-tuple-element.8.refs_4_.refs_8_.refs_9_.refs_7_, ...), custom_call_target="tpu_custom_call", output_to_operand_aliasing={{}: (8, {})} | custom-call | flops 4294967296 | bytes 2097152 | tf_op jit(solution)/shard_map/lags_2/pallas_call | solution.py:331
  (1 shorter events, 0.0 us)
Async XLA Ops:
  0.0 23.8 %copy-start = (f32[16,512]{1,0:T(8,128)S(1)}, f32[16,512]{1,0:T(8,128)}, u32[]{:S(2)}) copy-start(f32[16,512]{1,0:T(8,128)} %constant.36.clone.refs_3_) | copy-start | bytes 98308
  0.0 23.8 %copy-start.1 = (f32[2,512]{1,0:T(2,128)S(1)}, f32[2,512]{1,0:T(2,128)}, u32[]{:S(2)}) copy-start(f32[2,512]{1,0:T(2,128)} %constant.35.clone.refs_2_) | copy-start | bytes 12292
  0.0 13.7 %copy-start.2 = (s32[3,2]{0,1:T(2,128)S(1)}, s32[3,2]{0,1:T(2,128)}, u32[]{:S(2)}) copy-start(s32[3,2]{0,1:T(2,128)} %param.9) | copy-start | bytes 76
  8.0 12.4 %collective-permute-start = (bf16[3,128,1024]{2,1,0:T(8,128)(2,1)S(1)}, bf16[3,128,1024]{2,1,0:T(8,128)(2,1)S(1)}, u32[]{:S(2)}, u32[]{:S(2)}) collective-permute-start(bf16[3,128,1024]{2,1,0:T(8,128)(2,1)S(1)} %get-tuple-element.8.refs_4_.refs_8_.refs_9_.refs_7_), channel_id=1, source_target_pairs={{0,1},{1,0},{2,3},{3,2},{4,5},{5,4},{6,7},{7,6},{8,9},{9,8},{10,11... | collective-permute-start | bytes 2359304 | tf_op jit(solution)/shard_map/ppermute | solution.py:378
  8.1 15.7 %collective-permute-start.3 = (bf16[128,1024]{1,0:T(8,128)(2,1)S(1)}, bf16[128,1024]{1,0:T(8,128)(2,1)S(1)}, u32[]{:S(2)}, u32[]{:S(2)}) collective-permute-start(bf16[128,1024]{1,0:T(8,128)(2,1)S(1)} %get-tuple-element.9), channel_id=1, source_target_pairs={{2,0},{3,1},{4,2},{5,3},{6,4},{7,5},{8,6},{9,7},{10,8},{11,9},{12,... | collective-permute-start | bytes 786440 | tf_op jit(solution)/shard_map/ppermute | solution.py:376
  10.6 13.3 %collective-permute-start.4 = (bf16[128,1024]{1,0:T(8,128)(2,1)S(1)}, bf16[128,1024]{1,0:T(8,128)(2,1)S(1)}, u32[]{:S(2)}, u32[]{:S(2)}) collective-permute-start(bf16[128,1024]{1,0:T(8,128)(2,1)S(1)} %get-tuple-element.10), channel_id=1, source_target_pairs={{2,1},{4,3},{6,5},{8,7},{10,9},{12,11},{14,13},{18,17},{20,19},{22... | collective-permute-start | bytes 786440 | tf_op jit(solution)/shard_map/ppermute | solution.py:377
  13.7 5.5 %collective-permute-start.1 = (s32[3,2]{0,1:T(2,128)S(1)}, s32[3,2]{0,1:T(2,128)S(1)}, u32[]{:S(2)}, u32[]{:S(2)}) collective-permute-start(s32[3,2]{0,1:T(2,128)S(1)} %copy-done.2), channel_id=1, source_target_pairs={{0,2},{1,3},{2,4},{3,5},{4,6},{5,7},{6,8},{7,9},{8,10},{9,11},{10,... | collective-permute-start | bytes 80 | tf_op jit(solution)/shard_map/ppermute | solution.py:374
  20.5 13.0 %collective-permute-start.2 = (bf16[128,1024]{1,0:T(8,128)(2,1)S(1)}, bf16[128,1024]{1,0:T(8,128)(2,1)S(1)}, u32[]{:S(2)}, u32[]{:S(2)}) collective-permute-start(bf16[128,1024]{1,0:T(8,128)(2,1)S(1)} %select_bitcast_fusion), channel_id=1, source_target_pairs={{2,0},{3,1},{4,2},{5,3},{6,4},{7,5},{8,6},{9,7},{10,8},{11,9},{12,... | collective-permute-start | bytes 786440 | tf_op jit(solution)/shard_map/ppermute | solution.py:379
where the time goes:
time: 39.2 us; the launch traced here: 39 us
  Pallas kernels  23 us (59%)
  starting transfers between devices  10.2 us (26%)
  waiting for transfers between devices  3.42 us (9%)
  between operations  1.61 us (4%)
  local copies, waits for them, and re-layouts  0.69 us (2%)
    pallas_call x2, Pallas kernels, corr_tiles(): pl.pallas_call(functools.partial(corr_kernel, slots, blocks, scale, coars...  15 us
    pallas_call x1, Pallas kernels, spectra(): pl.pallas_call(functools.partial(spectra_kernel, blocks, wins), out_shape...  8.02 us
    ppermute x1, waiting for transfers between devices, body(): want = lax.ppermute(tile_pairs, 'tile', behind2)[blocks - 1, 1]  3.41 us
    ppermute x1, starting transfers between devices, body(): far2 = lax.ppermute(chosen(want, everything, other), 'tile', ahead2)  3.33 us
    ppermute x1, starting transfers between devices, body(): near1 = lax.ppermute(w1, 'tile', across)  3.12 us
    ppermute x1, starting transfers between devices, body(): far0 = lax.ppermute(w0, 'tile', ahead2)  2.43 us
    ppermute x1, starting transfers between devices, body(): want = lax.ppermute(tile_pairs, 'tile', behind2)[blocks - 1, 1]  1.29 us
  transfers between devices with their start and end apart: 5, of which 1 were waited for; matrix products, arithmetic and copies ran while one was open for 2% of the time, Pallas kernels for 25%

commit v1 on v0

--- a/solution.py
+++ b/solution.py
@@ -77,15 +77,11 @@
                 left[2 * b, place[0], place[1]] = (head + tail).astype(BF16)
                 left[2 * b + 1, place[0], place[1]] = (head - tail).astype(BF16)
 
-    def finish(b):
-        spec = [
-            jnp.dot(
-                left[2 * b + sign],
-                tab[sign * half : (sign + 1) * half, :],
-                preferred_element_type=F32,
-            )
-            for sign in range(2)
-        ]
+    def product(b, sign):
+        table = tab[sign * half : (sign + 1) * half, :]
+        return jnp.dot(left[2 * b + sign], table, preferred_element_type=F32)
+
+    def finish(b, spec):
         mean = tab[2 * half :, :]
         energy = [s[:, :128] * s[:, :128] + s[:, 128:] * s[:, 128:] for s in spec]
         energy = jnp.concatenate(energy, 1)
@@ -113,10 +109,12 @@
     for b in range(1, blocks):
         x_copy(2 * b).wait()
         x_copy(2 * b + 1).wait()
-        finish(b - 1)
+        even = product(b - 1, 0)
         fold(b, 0)
+        odd = product(b - 1, 1)
         fold(b, 1)
-    finish(blocks - 1)
+        finish(b - 1, [even, odd])
+    finish(blocks - 1, [product(blocks - 1, sign) for sign in range(2)])
 
 
 def spectra(view, table, blocks, wins):

time: 39.2 us -> 39.2 us (level)
  no operation moved by 1% of the time
where the time goes in v1:
time: 39.2 us; the launch traced here: 39 us
  Pallas kernels  23 us (59%)
  starting transfers between devices  10.2 us (26%)
  waiting for transfers between devices  3.42 us (9%)
  between operations  1.61 us (4%)
  local copies, waits for them, and re-layouts  0.69 us (2%)
    pallas_call x2, Pallas kernels, corr_tiles(): pl.pallas_call(functools.partial(corr_kernel, slots, blocks, scale, coars...  15 us
    pallas_call x1, Pallas kernels, spectra(): pl.pallas_call(functools.partial(spectra_kernel, blocks, wins), out_shape...  8.02 us
    ppermute x1, waiting for transfers between devices, body(): want = lax.ppermute(tile_pairs, 'tile', behind2)[blocks - 1, 1]  3.41 us
    ppermute x1, starting transfers between devices, body(): far2 = lax.ppermute(chosen(want, everything, other), 'tile', ahead2)  3.33 us
    ppermute x1, starting transfers between devices, body(): near1 = lax.ppermute(w1, 'tile', across)  3.12 us
    ppermute x1, starting transfers between devices, body(): far0 = lax.ppermute(w0, 'tile', ahead2)  2.43 us
    ppermute x1, starting transfers between devices, body(): want = lax.ppermute(tile_pairs, 'tile', behind2)[blocks - 1, 1]  1.29 us
  transfers between devices with their start and end apart: 5, of which 1 were waited for; matrix products, arithmetic and copies ran while one was open for 2% of the time, Pallas kernels for 25%

profile of v1, /device:TPU:28, one launch (start us, length us, event | category | flops | bytes accessed | tf_op | source)
XLA Modules:
  0.0 39.0 jit_solution(9160502998382674426)
XLA Ops:
  0.0 0.0 copy-start
  0.0 0.0 copy-start.1
  0.0 0.0 copy-start.2
  0.0 8.0 %spectra.1 = (bf16[128,1024]{1,0:T(8,128)(2,1)S(1)}, bf16[128,1024]{1,0:T(8,128)(2,1)S(1)}, bf16[3,128,1024]{2,1,0:T(8,128)(2,1)S(1)}) custom-call(bf16[384,64,128]{2,1,0:T(8,128)(2,1)} %bitcast.8, bf16[4352,256]{1,0:T(8,128)(2,1)} %constant.34.clone.tab_hbm), custom_call_target="tpu_custom_call" | custom-call | flops 1610612736 | bytes 8388608 | tf_op jit(solution)/shard_map/spectra/pallas_call | solution.py:123
  8.0 0.1 collective-permute-start
  8.1 2.4 %collective-permute-start.3 = (bf16[128,1024]{1,0:T(8,128)(2,1)S(1)}, bf16[128,1024]{1,0:T(8,128)(2,1)S(1)}, u32[]{:S(2)}, u32[]{:S(2)}) collective-permute-start(bf16[128,1024]{1,0:T(8,128)(2,1)S(1)} %get-tuple-element.9), channel_id=1, source_target_pairs={{2,0},{3,1},{4,2},{5,3},{6,4},{7,5},{8,6},{9,7},{10,8},{11,9},{12,... | collective-permute-start | bytes 786440 | tf_op jit(solution)/shard_map/ppermute | solution.py:374
  10.6 3.1 %collective-permute-start.4 = (bf16[128,1024]{1,0:T(8,128)(2,1)S(1)}, bf16[128,1024]{1,0:T(8,128)(2,1)S(1)}, u32[]{:S(2)}, u32[]{:S(2)}) collective-permute-start(bf16[128,1024]{1,0:T(8,128)(2,1)S(1)} %get-tuple-element.10), channel_id=1, source_target_pairs={{2,1},{4,3},{6,5},{8,7},{10,9},{12,11},{14,13},{18,17},{20,19},{22... | collective-permute-start | bytes 786440 | tf_op jit(solution)/shard_map/ppermute | solution.py:375
  13.7 0.0 copy-done.2
  13.7 1.3 %collective-permute-start.1 = (s32[3,2]{0,1:T(2,128)S(1)}, s32[3,2]{0,1:T(2,128)S(1)}, u32[]{:S(2)}, u32[]{:S(2)}) collective-permute-start(s32[3,2]{0,1:T(2,128)S(1)} %copy-done.2), channel_id=1, source_target_pairs={{0,2},{1,3},{2,4},{3,5},{4,6},{5,7},{6,8},{7,9},{8,10},{9,11},{10,... | collective-permute-start | bytes 80 | tf_op jit(solution)/shard_map/ppermute | solution.py:372
  15.0 0.1 copy.12.refs_0_
  15.7 3.4 %collective-permute-done.1 = s32[3,2]{0,1:T(2,128)S(1)} collective-permute-done((s32[3,2]{0,1:T(2,128)S(1)}, s32[3,2]{0,1:T(2,128)S(1)}, u32[]{:S(2)}, u32[]{:S(2)}) %collective-permute-start.1) | collective-permute-done | bytes 56 | tf_op jit(solution)/shard_map/ppermute | solution.py:372
  19.2 0.6 %slice.3 = s32[1,1]{0,1:T(1,128)} slice(s32[3,2]{0,1:T(2,128)S(1)} %collective-permute-done.1), slice={[2:3], [1:2]} | slice | bytes 8 | tf_op jit(solution)/shard_map/slice | solution.py:372
  20.4 0.0 collective-permute-done.refs_5_
  20.5 3.3 %collective-permute-start.2 = (bf16[128,1024]{1,0:T(8,128)(2,1)S(1)}, bf16[128,1024]{1,0:T(8,128)(2,1)S(1)}, u32[]{:S(2)}, u32[]{:S(2)}) collective-permute-start(bf16[128,1024]{1,0:T(8,128)(2,1)S(1)} %select_bitcast_fusion), channel_id=1, source_target_pairs={{2,0},{3,1},{4,2},{5,3},{6,4},{7,5},{8,6},{9,7},{10,8},{11,9},{12,... | collective-permute-start | bytes 786440 | tf_op jit(solution)/shard_map/ppermute | solution.py:377
  23.8 0.0 collective-permute-done.3.refs_6_
  23.8 0.0 collective-permute-done.4.refs_7_
  23.8 0.0 copy-done
  23.8 0.0 copy-done.1
  23.8 9.6 %lags_0_1.1.refs_8_ = bf16[3,128,8192]{2,1,0:T(8,128)(2,1)} custom-call(s32[3,2]{1,0:T(4,128)S(1)} %copy.12.refs_0_, s32[1]{0:T(128)S(6)} %copy.14.refs_1_, f32[2,512]{1,0:T(2,128)S(1)} %copy-done.1, f32[16,512]{1,0:T(8,128)S(1)} %copy-done, bf16[3,128,1024]{2,1,0:T(8,128)(2,1)S(1)} %get-tuple-element.8.refs_4_.refs_8_.refs_9_.refs_7_, ...), custom_call_target="tpu_custom_call" | custom-call | flops 8589934592 | bytes 4194304 | tf_op jit(solution)/shard_map/lags_0_1/pallas_call | solution.py:329
  33.5 0.0 collective-permute-done.2.refs_6_
  33.5 5.4 %lags_2.1 = bf16[3,128,8192]{2,1,0:T(8,128)(2,1)} custom-call(s32[3,2]{1,0:T(4,128)S(1)} %copy.12.refs_0_, s32[1]{0:T(128)S(6)} %copy.14.refs_1_, f32[2,512]{1,0:T(2,128)S(1)} %copy-done.1, f32[16,512]{1,0:T(8,128)S(1)} %copy-done, bf16[3,128,1024]{2,1,0:T(8,128)(2,1)S(1)} %get-tuple-element.8.refs_4_.refs_8_.refs_9_.refs_7_, ...), custom_call_target="tpu_custom_call", output_to_operand_aliasing={{}: (8, {})} | custom-call | flops 4294967296 | bytes 2097152 | tf_op jit(solution)/shard_map/lags_2/pallas_call | solution.py:329
  (1 shorter events, 0.0 us)
Async XLA Ops:
  0.0 23.8 %copy-start = (f32[16,512]{1,0:T(8,128)S(1)}, f32[16,512]{1,0:T(8,128)}, u32[]{:S(2)}) copy-start(f32[16,512]{1,0:T(8,128)} %constant.36.clone.refs_3_) | copy-start | bytes 98308
  0.0 23.8 %copy-start.1 = (f32[2,512]{1,0:T(2,128)S(1)}, f32[2,512]{1,0:T(2,128)}, u32[]{:S(2)}) copy-start(f32[2,512]{1,0:T(2,128)} %constant.35.clone.refs_2_) | copy-start | bytes 12292
  0.0 13.7 %copy-start.2 = (s32[3,2]{0,1:T(2,128)S(1)}, s32[3,2]{0,1:T(2,128)}, u32[]{:S(2)}) copy-start(s32[3,2]{0,1:T(2,128)} %param.9) | copy-start | bytes 76
  8.0 12.4 %collective-permute-start = (bf16[3,128,1024]{2,1,0:T(8,128)(2,1)S(1)}, bf16[3,128,1024]{2,1,0:T(8,128)(2,1)S(1)}, u32[]{:S(2)}, u32[]{:S(2)}) collective-permute-start(bf16[3,128,1024]{2,1,0:T(8,128)(2,1)S(1)} %get-tuple-element.8.refs_4_.refs_8_.refs_9_.refs_7_), channel_id=1, source_target_pairs={{0,1},{1,0},{2,3},{3,2},{4,5},{5,4},{6,7},{7,6},{8,9},{9,8},{10,11... | collective-permute-start | bytes 2359304 | tf_op jit(solution)/shard_map/ppermute | solution.py:376
  8.1 15.7 %collective-permute-start.3 = (bf16[128,1024]{1,0:T(8,128)(2,1)S(1)}, bf16[128,1024]{1,0:T(8,128)(2,1)S(1)}, u32[]{:S(2)}, u32[]{:S(2)}) collective-permute-start(bf16[128,1024]{1,0:T(8,128)(2,1)S(1)} %get-tuple-element.9), channel_id=1, source_target_pairs={{2,0},{3,1},{4,2},{5,3},{6,4},{7,5},{8,6},{9,7},{10,8},{11,9},{12,... | collective-permute-start | bytes 786440 | tf_op jit(solution)/shard_map/ppermute | solution.py:374
  10.6 13.3 %collective-permute-start.4 = (bf16[128,1024]{1,0:T(8,128)(2,1)S(1)}, bf16[128,1024]{1,0:T(8,128)(2,1)S(1)}, u32[]{:S(2)}, u32[]{:S(2)}) collective-permute-start(bf16[128,1024]{1,0:T(8,128)(2,1)S(1)} %get-tuple-element.10), channel_id=1, source_target_pairs={{2,1},{4,3},{6,5},{8,7},{10,9},{12,11},{14,13},{18,17},{20,19},{22... | collective-permute-start | bytes 786440 | tf_op jit(solution)/shard_map/ppermute | solution.py:375
  13.7 5.5 %collective-permute-start.1 = (s32[3,2]{0,1:T(2,128)S(1)}, s32[3,2]{0,1:T(2,128)S(1)}, u32[]{:S(2)}, u32[]{:S(2)}) collective-permute-start(s32[3,2]{0,1:T(2,128)S(1)} %copy-done.2), channel_id=1, source_target_pairs={{0,2},{1,3},{2,4},{3,5},{4,6},{5,7},{6,8},{7,9},{8,10},{9,11},{10,... | collective-permute-start | bytes 80 | tf_op jit(solution)/shard_map/ppermute | solution.py:372
  20.5 13.0 %collective-permute-start.2 = (bf16[128,1024]{1,0:T(8,128)(2,1)S(1)}, bf16[128,1024]{1,0:T(8,128)(2,1)S(1)}, u32[]{:S(2)}, u32[]{:S(2)}) collective-permute-start(bf16[128,1024]{1,0:T(8,128)(2,1)S(1)} %select_bitcast_fusion), channel_id=1, source_target_pairs={{2,0},{3,1},{4,2},{5,3},{6,4},{7,5},{8,6},{9,7},{10,8},{11,9},{12,... | collective-permute-start | bytes 786440 | tf_op jit(solution)/shard_map/ppermute | solution.py:377

commit v2 on v1

--- a/solution.py
+++ b/solution.py
@@ -154,9 +154,9 @@
     return jnp.where(jnp.logical_or(index >= 0, me % 2 == 0), own, beside)
 
 
-def corr_kernel(slots, blocks, scale, coarse, *refs):
+def corr_kernel(slots, blocks, scale, coarse, width, *refs):
     fine = LAGS // coarse
-    js = 256 // fine
+    js = width // fine
     chunks = CH // js
     count = len(slots)
     pairs_ref, count_ref, atab_ref, btab_ref, all_ref, other_ref = refs[:6]
@@ -247,7 +247,7 @@
     lane = lax.broadcasted_iota(jnp.int32, (CH, 128), 1)
 
     def arrange(n, c, prod):
-        for v in range(2):
+        for v in range(width // 128):
             x = [prod[a * CH : (a + 1) * CH, v * 128 : (v + 1) * 128] for a in range(coarse)]
             bit = 1
             while bit < coarse:
@@ -306,10 +306,10 @@
             out_copy(n, c).wait()
 
 
-def corr_tiles(slots, scale, coarse, pairs, tile_count, everything, other, fars, buffer):
+def corr_tiles(slots, width, scale, coarse, pairs, tile_count, everything, other, fars, buffer):
     fine = LAGS // coarse
     tables = [jnp.asarray(t) for t in phase_tables(coarse, scale)]
-    js = 256 // fine
+    js = width // fine
     chunks = CH // js
     count = len(slots)
     blocks, _, depth = everything.shape
@@ -327,7 +327,7 @@
         operands.append(buffer)
         in_specs.append(pl.BlockSpec(memory_space=pl.ANY))
     return pl.pallas_call(
-        functools.partial(corr_kernel, slots, blocks, scale, coarse),
+        functools.partial(corr_kernel, slots, blocks, scale, coarse, width),
         grid=(1,),
         out_shape=jax.ShapeDtypeStruct((blocks, CH, CH * LAGS), BF16),
         in_specs=in_specs,
@@ -376,8 +376,8 @@
     other = lax.ppermute(everything, "tile", swap)
     far2 = lax.ppermute(chosen(want, everything, other), "tile", ahead2)
     shared = (scale, 4, tile_pairs, tile_count, everything, other)
-    out = corr_tiles((0, 1), *shared, (far0, near1), None)
-    return corr_tiles((2,), *shared, (far2,), out)
+    out = corr_tiles((0, 1), 512, *shared, (far0, near1), None)
+    return corr_tiles((2,), 256, *shared, (far2,), out)
 
 
 def solution(mesh):

time: 39.2 us -> 38.6 us (0.985)
  the two profiles are of different devices: /device:TPU:28 before, /device:TPU:26 now
where the time goes in v2:
time: 38.6 us; the launch traced here: 38.4 us
  Pallas kernels  22.4 us (58%)
  starting transfers between devices  11.5 us (30%)
  waiting for transfers between devices  2.18 us (6%)
  between operations  1.61 us (4%)
  local copies, waits for them, and re-layouts  0.69 us (2%)
    pallas_call x2, Pallas kernels, corr_tiles(): pl.pallas_call(functools.partial(corr_kernel, slots, blocks, scale, coars...  14.4 us
    pallas_call x1, Pallas kernels, spectra(): pl.pallas_call(functools.partial(spectra_kernel, blocks, wins), out_shape...  8.02 us
    ppermute x1, starting transfers between devices, body(): want = lax.ppermute(tile_pairs, 'tile', behind2)[blocks - 1, 1]  3.43 us
    ppermute x1, starting transfers between devices, body(): far0 = lax.ppermute(w0, 'tile', ahead2)  3.31 us
    ppermute x1, starting transfers between devices, body(): far2 = lax.ppermute(chosen(want, everything, other), 'tile', ahead2)  2.46 us
    ppermute x1, starting transfers between devices, body(): near1 = lax.ppermute(w1, 'tile', across)  2.24 us
    ppermute x1, waiting for transfers between devices, body(): want = lax.ppermute(tile_pairs, 'tile', behind2)[blocks - 1, 1]  2.17 us
  transfers between devices with their start and end apart: 5, of which 1 were waited for; matrix products, arithmetic and copies ran while one was open for 2% of the time, Pallas kernels for 24%

profile of v2, /device:TPU:26, one launch (start us, length us, event | category | flops | bytes accessed | tf_op | source)
XLA Modules:
  0.0 38.4 jit_solution(8913233802576124876)
XLA Ops:
  0.0 0.0 copy-start
  0.0 0.0 copy-start.1
  0.0 0.0 copy-start.2
  0.0 8.0 %spectra.1 = (bf16[128,1024]{1,0:T(8,128)(2,1)S(1)}, bf16[128,1024]{1,0:T(8,128)(2,1)S(1)}, bf16[3,128,1024]{2,1,0:T(8,128)(2,1)S(1)}) custom-call(bf16[384,64,128]{2,1,0:T(8,128)(2,1)} %bitcast.8, bf16[4352,256]{1,0:T(8,128)(2,1)} %constant.34.clone.tab_hbm), custom_call_target="tpu_custom_call" | custom-call | flops 1610612736 | bytes 8388608 | tf_op jit(solution)/shard_map/spectra/pallas_call | solution.py:123
  8.0 0.1 collective-permute-start
  8.1 3.3 %collective-permute-start.3 = (bf16[128,1024]{1,0:T(8,128)(2,1)S(1)}, bf16[128,1024]{1,0:T(8,128)(2,1)S(1)}, u32[]{:S(2)}, u32[]{:S(2)}) collective-permute-start(bf16[128,1024]{1,0:T(8,128)(2,1)S(1)} %get-tuple-element.9), channel_id=1, source_target_pairs={{2,0},{3,1},{4,2},{5,3},{6,4},{7,5},{8,6},{9,7},{10,8},{11,9},{12,... | collective-permute-start | bytes 786440 | tf_op jit(solution)/shard_map/ppermute | solution.py:374
  11.4 2.2 %collective-permute-start.4 = (bf16[128,1024]{1,0:T(8,128)(2,1)S(1)}, bf16[128,1024]{1,0:T(8,128)(2,1)S(1)}, u32[]{:S(2)}, u32[]{:S(2)}) collective-permute-start(bf16[128,1024]{1,0:T(8,128)(2,1)S(1)} %get-tuple-element.10), channel_id=1, source_target_pairs={{2,1},{4,3},{6,5},{8,7},{10,9},{12,11},{14,13},{18,17},{20,19},{22... | collective-permute-start | bytes 786440 | tf_op jit(solution)/shard_map/ppermute | solution.py:375
  13.7 0.0 copy-done.2
  13.7 3.4 %collective-permute-start.1 = (s32[3,2]{0,1:T(2,128)S(1)}, s32[3,2]{0,1:T(2,128)S(1)}, u32[]{:S(2)}, u32[]{:S(2)}) collective-permute-start(s32[3,2]{0,1:T(2,128)S(1)} %copy-done.2), channel_id=1, source_target_pairs={{0,2},{1,3},{2,4},{3,5},{4,6},{5,7},{6,8},{7,9},{8,10},{9,11},{10,... | collective-permute-start | bytes 80 | tf_op jit(solution)/shard_map/ppermute | solution.py:372
  17.1 0.1 copy.12.refs_0_
  17.9 2.2 %collective-permute-done.1 = s32[3,2]{0,1:T(2,128)S(1)} collective-permute-done((s32[3,2]{0,1:T(2,128)S(1)}, s32[3,2]{0,1:T(2,128)S(1)}, u32[]{:S(2)}, u32[]{:S(2)}) %collective-permute-start.1) | collective-permute-done | bytes 56 | tf_op jit(solution)/shard_map/ppermute | solution.py:372
  20.1 0.6 %slice.3 = s32[1,1]{0,1:T(1,128)} slice(s32[3,2]{0,1:T(2,128)S(1)} %collective-permute-done.1), slice={[2:3], [1:2]} | slice | bytes 8 | tf_op jit(solution)/shard_map/slice | solution.py:372
  21.3 0.0 collective-permute-done.refs_5_
  21.4 2.5 %collective-permute-start.2 = (bf16[128,1024]{1,0:T(8,128)(2,1)S(1)}, bf16[128,1024]{1,0:T(8,128)(2,1)S(1)}, u32[]{:S(2)}, u32[]{:S(2)}) collective-permute-start(bf16[128,1024]{1,0:T(8,128)(2,1)S(1)} %select_bitcast_fusion), channel_id=1, source_target_pairs={{2,0},{3,1},{4,2},{5,3},{6,4},{7,5},{8,6},{9,7},{10,8},{11,9},{12,... | collective-permute-start | bytes 786440 | tf_op jit(solution)/shard_map/ppermute | solution.py:377
  23.8 0.0 collective-permute-done.3.refs_6_
  23.8 0.0 collective-permute-done.4.refs_7_
  23.8 0.0 copy-done
  23.9 0.0 copy-done.1
  23.9 9.0 %lags_0_1.1.refs_8_ = bf16[3,128,8192]{2,1,0:T(8,128)(2,1)} custom-call(s32[3,2]{1,0:T(4,128)S(1)} %copy.12.refs_0_, s32[1]{0:T(128)S(6)} %copy.14.refs_1_, f32[2,512]{1,0:T(2,128)S(1)} %copy-done.1, f32[16,512]{1,0:T(8,128)S(1)} %copy-done, bf16[3,128,1024]{2,1,0:T(8,128)(2,1)S(1)} %get-tuple-element.8.refs_4_.refs_8_.refs_9_.refs_7_, ...), custom_call_target="tpu_custom_call" | custom-call | flops 8589934592 | bytes 4194304 | tf_op jit(solution)/shard_map/lags_0_1/pallas_call | solution.py:329
  32.9 0.0 collective-permute-done.2.refs_6_
  32.9 5.4 %lags_2.1 = bf16[3,128,8192]{2,1,0:T(8,128)(2,1)} custom-call(s32[3,2]{1,0:T(4,128)S(1)} %copy.12.refs_0_, s32[1]{0:T(128)S(6)} %copy.14.refs_1_, f32[2,512]{1,0:T(2,128)S(1)} %copy-done.1, f32[16,512]{1,0:T(8,128)S(1)} %copy-done, bf16[3,128,1024]{2,1,0:T(8,128)(2,1)S(1)} %get-tuple-element.8.refs_4_.refs_8_.refs_9_.refs_7_, ...), custom_call_target="tpu_custom_call", output_to_operand_aliasing={{}: (8, {})} | custom-call | flops 4294967296 | bytes 2097152 | tf_op jit(solution)/shard_map/lags_2/pallas_call | solution.py:329
  (1 shorter events, 0.0 us)
Async XLA Ops:
  0.0 23.8 %copy-start = (f32[16,512]{1,0:T(8,128)S(1)}, f32[16,512]{1,0:T(8,128)}, u32[]{:S(2)}) copy-start(f32[16,512]{1,0:T(8,128)} %constant.36.clone.refs_3_) | copy-start | bytes 98308
  0.0 23.9 %copy-start.1 = (f32[2,512]{1,0:T(2,128)S(1)}, f32[2,512]{1,0:T(2,128)}, u32[]{:S(2)}) copy-start(f32[2,512]{1,0:T(2,128)} %constant.35.clone.refs_2_) | copy-start | bytes 12292
  0.0 13.7 %copy-start.2 = (s32[3,2]{0,1:T(2,128)S(1)}, s32[3,2]{0,1:T(2,128)}, u32[]{:S(2)}) copy-start(s32[3,2]{0,1:T(2,128)} %param.9) | copy-start | bytes 76
  8.0 13.3 %collective-permute-start = (bf16[3,128,1024]{2,1,0:T(8,128)(2,1)S(1)}, bf16[3,128,1024]{2,1,0:T(8,128)(2,1)S(1)}, u32[]{:S(2)}, u32[]{:S(2)}) collective-permute-start(bf16[3,128,1024]{2,1,0:T(8,128)(2,1)S(1)} %get-tuple-element.8.refs_4_.refs_8_.refs_9_.refs_7_), channel_id=1, source_target_pairs={{0,1},{1,0},{2,3},{3,2},{4,5},{5,4},{6,7},{7,6},{8,9},{9,8},{10,11... | collective-permute-start | bytes 2359304 | tf_op jit(solution)/shard_map/ppermute | solution.py:376
  8.1 15.7 %collective-permute-start.3 = (bf16[128,1024]{1,0:T(8,128)(2,1)S(1)}, bf16[128,1024]{1,0:T(8,128)(2,1)S(1)}, u32[]{:S(2)}, u32[]{:S(2)}) collective-permute-start(bf16[128,1024]{1,0:T(8,128)(2,1)S(1)} %get-tuple-element.9), channel_id=1, source_target_pairs={{2,0},{3,1},{4,2},{5,3},{6,4},{7,5},{8,6},{9,7},{10,8},{11,9},{12,... | collective-permute-start | bytes 786440 | tf_op jit(solution)/shard_map/ppermute | solution.py:374
  11.4 12.4 %collective-permute-start.4 = (bf16[128,1024]{1,0:T(8,128)(2,1)S(1)}, bf16[128,1024]{1,0:T(8,128)(2,1)S(1)}, u32[]{:S(2)}, u32[]{:S(2)}) collective-permute-start(bf16[128,1024]{1,0:T(8,128)(2,1)S(1)} %get-tuple-element.10), channel_id=1, source_target_pairs={{2,1},{4,3},{6,5},{8,7},{10,9},{12,11},{14,13},{18,17},{20,19},{22... | collective-permute-start | bytes 786440 | tf_op jit(solution)/shard_map/ppermute | solution.py:375
  13.7 6.4 %collective-permute-start.1 = (s32[3,2]{0,1:T(2,128)S(1)}, s32[3,2]{0,1:T(2,128)S(1)}, u32[]{:S(2)}, u32[]{:S(2)}) collective-permute-start(s32[3,2]{0,1:T(2,128)S(1)} %copy-done.2), channel_id=1, source_target_pairs={{0,2},{1,3},{2,4},{3,5},{4,6},{5,7},{6,8},{7,9},{8,10},{9,11},{10,... | collective-permute-start | bytes 80 | tf_op jit(solution)/shard_map/ppermute | solution.py:372
  21.4 11.6 %collective-permute-start.2 = (bf16[128,1024]{1,0:T(8,128)(2,1)S(1)}, bf16[128,1024]{1,0:T(8,128)(2,1)S(1)}, u32[]{:S(2)}, u32[]{:S(2)}) collective-permute-start(bf16[128,1024]{1,0:T(8,128)(2,1)S(1)} %select_bitcast_fusion), channel_id=1, source_target_pairs={{2,0},{3,1},{4,2},{5,3},{6,4},{7,5},{8,6},{9,7},{10,8},{11,9},{12,... | collective-permute-start | bytes 786440 | tf_op jit(solution)/shard_map/ppermute | solution.py:377

commit v3 on v2

--- a/solution.py
+++ b/solution.py
@@ -377,7 +377,7 @@
     far2 = lax.ppermute(chosen(want, everything, other), "tile", ahead2)
     shared = (scale, 4, tile_pairs, tile_count, everything, other)
     out = corr_tiles((0, 1), 512, *shared, (far0, near1), None)
-    return corr_tiles((2,), 256, *shared, (far2,), out)
+    return corr_tiles((2,), 512, *shared, (far2,), out)
 
 
 def solution(mesh):

time: 38.6 us -> 38.7 us (level)
  the two profiles are of different devices: /device:TPU:26 before, /device:TPU:28 now
where the time goes in v3:
time: 38.7 us; the launch traced here: 38.5 us
  Pallas kernels  22.5 us (58%)
  starting transfers between devices  10.2 us (26%)
  waiting for transfers between devices  3.42 us (9%)
  between operations  1.61 us (4%)
  local copies, waits for them, and re-layouts  0.69 us (2%)
    pallas_call x2, Pallas kernels, corr_tiles(): pl.pallas_call(functools.partial(corr_kernel, slots, blocks, scale, coars...  14.5 us
    pallas_call x1, Pallas kernels, spectra(): pl.pallas_call(functools.partial(spectra_kernel, blocks, wins), out_shape...  8.02 us
    ppermute x1, waiting for transfers between devices, body(): want = lax.ppermute(tile_pairs, 'tile', behind2)[blocks - 1, 1]  3.41 us
    ppermute x1, starting transfers between devices, body(): far2 = lax.ppermute(chosen(want, everything, other), 'tile', ahead2)  3.33 us
    ppermute x1, starting transfers between devices, body(): near1 = lax.ppermute(w1, 'tile', across)  3.12 us
    ppermute x1, starting transfers between devices, body(): far0 = lax.ppermute(w0, 'tile', ahead2)  2.43 us
    ppermute x1, starting transfers between devices, body(): want = lax.ppermute(tile_pairs, 'tile', behind2)[blocks - 1, 1]  1.29 us
  transfers between devices with their start and end apart: 5, of which 1 were waited for; matrix products, arithmetic and copies ran while one was open for 2% of the time, Pallas kernels for 23%

profile of v3, /device:TPU:28, one launch (start us, length us, event | category | flops | bytes accessed | tf_op | source)
XLA Modules:
  0.0 38.5 jit_solution(12811941511062073660)
XLA Ops:
  0.0 0.0 copy-start
  0.0 0.0 copy-start.1
  0.0 0.0 copy-start.2
  0.0 8.0 %spectra.1 = (bf16[128,1024]{1,0:T(8,128)(2,1)S(1)}, bf16[128,1024]{1,0:T(8,128)(2,1)S(1)}, bf16[3,128,1024]{2,1,0:T(8,128)(2,1)S(1)}) custom-call(bf16[384,64,128]{2,1,0:T(8,128)(2,1)} %bitcast.8, bf16[4352,256]{1,0:T(8,128)(2,1)} %constant.34.clone.tab_hbm), custom_call_target="tpu_custom_call" | custom-call | flops 1610612736 | bytes 8388608 | tf_op jit(solution)/shard_map/spectra/pallas_call | solution.py:123
  8.0 0.1 collective-permute-start
  8.1 2.4 %collective-permute-start.3 = (bf16[128,1024]{1,0:T(8,128)(2,1)S(1)}, bf16[128,1024]{1,0:T(8,128)(2,1)S(1)}, u32[]{:S(2)}, u32[]{:S(2)}) collective-permute-start(bf16[128,1024]{1,0:T(8,128)(2,1)S(1)} %get-tuple-element.9), channel_id=1, source_target_pairs={{2,0},{3,1},{4,2},{5,3},{6,4},{7,5},{8,6},{9,7},{10,8},{11,9},{12,... | collective-permute-start | bytes 786440 | tf_op jit(solution)/shard_map/ppermute | solution.py:374
  10.6 3.1 %collective-permute-start.4 = (bf16[128,1024]{1,0:T(8,128)(2,1)S(1)}, bf16[128,1024]{1,0:T(8,128)(2,1)S(1)}, u32[]{:S(2)}, u32[]{:S(2)}) collective-permute-start(bf16[128,1024]{1,0:T(8,128)(2,1)S(1)} %get-tuple-element.10), channel_id=1, source_target_pairs={{2,1},{4,3},{6,5},{8,7},{10,9},{12,11},{14,13},{18,17},{20,19},{22... | collective-permute-start | bytes 786440 | tf_op jit(solution)/shard_map/ppermute | solution.py:375
  13.7 0.0 copy-done.2
  13.7 1.3 %collective-permute-start.1 = (s32[3,2]{0,1:T(2,128)S(1)}, s32[3,2]{0,1:T(2,128)S(1)}, u32[]{:S(2)}, u32[]{:S(2)}) collective-permute-start(s32[3,2]{0,1:T(2,128)S(1)} %copy-done.2), channel_id=1, source_target_pairs={{0,2},{1,3},{2,4},{3,5},{4,6},{5,7},{6,8},{7,9},{8,10},{9,11},{10,... | collective-permute-start | bytes 80 | tf_op jit(solution)/shard_map/ppermute | solution.py:372
  15.0 0.1 copy.12.refs_0_
  15.7 3.4 %collective-permute-done.1 = s32[3,2]{0,1:T(2,128)S(1)} collective-permute-done((s32[3,2]{0,1:T(2,128)S(1)}, s32[3,2]{0,1:T(2,128)S(1)}, u32[]{:S(2)}, u32[]{:S(2)}) %collective-permute-start.1) | collective-permute-done | bytes 56 | tf_op jit(solution)/shard_map/ppermute | solution.py:372
  19.2 0.6 %slice.3 = s32[1,1]{0,1:T(1,128)} slice(s32[3,2]{0,1:T(2,128)S(1)} %collective-permute-done.1), slice={[2:3], [1:2]} | slice | bytes 8 | tf_op jit(solution)/shard_map/slice | solution.py:372
  20.4 0.0 collective-permute-done.refs_5_
  20.5 3.3 %collective-permute-start.2 = (bf16[128,1024]{1,0:T(8,128)(2,1)S(1)}, bf16[128,1024]{1,0:T(8,128)(2,1)S(1)}, u32[]{:S(2)}, u32[]{:S(2)}) collective-permute-start(bf16[128,1024]{1,0:T(8,128)(2,1)S(1)} %select_bitcast_fusion), channel_id=1, source_target_pairs={{2,0},{3,1},{4,2},{5,3},{6,4},{7,5},{8,6},{9,7},{10,8},{11,9},{12,... | collective-permute-start | bytes 786440 | tf_op jit(solution)/shard_map/ppermute | solution.py:377
  23.8 0.0 collective-permute-done.3.refs_6_
  23.8 0.0 collective-permute-done.4.refs_7_
  23.8 0.0 copy-done
  23.8 0.0 copy-done.1
  23.8 9.0 %lags_0_1.1.refs_8_ = bf16[3,128,8192]{2,1,0:T(8,128)(2,1)} custom-call(s32[3,2]{1,0:T(4,128)S(1)} %copy.12.refs_0_, s32[1]{0:T(128)S(6)} %copy.14.refs_1_, f32[2,512]{1,0:T(2,128)S(1)} %copy-done.1, f32[16,512]{1,0:T(8,128)S(1)} %copy-done, bf16[3,128,1024]{2,1,0:T(8,128)(2,1)S(1)} %get-tuple-element.8.refs_4_.refs_8_.refs_9_.refs_7_, ...), custom_call_target="tpu_custom_call" | custom-call | flops 8589934592 | bytes 4194304 | tf_op jit(solution)/shard_map/lags_0_1/pallas_call | solution.py:329
  32.9 0.0 collective-permute-done.2.refs_6_
  32.9 5.4 %lags_2.1 = bf16[3,128,8192]{2,1,0:T(8,128)(2,1)} custom-call(s32[3,2]{1,0:T(4,128)S(1)} %copy.12.refs_0_, s32[1]{0:T(128)S(6)} %copy.14.refs_1_, f32[2,512]{1,0:T(2,128)S(1)} %copy-done.1, f32[16,512]{1,0:T(8,128)S(1)} %copy-done, bf16[3,128,1024]{2,1,0:T(8,128)(2,1)S(1)} %get-tuple-element.8.refs_4_.refs_8_.refs_9_.refs_7_, ...), custom_call_target="tpu_custom_call", output_to_operand_aliasing={{}: (8, {})} | custom-call | flops 4294967296 | bytes 2097152 | tf_op jit(solution)/shard_map/lags_2/pallas_call | solution.py:329
  (1 shorter events, 0.0 us)
Async XLA Ops:
  0.0 23.8 %copy-start = (f32[16,512]{1,0:T(8,128)S(1)}, f32[16,512]{1,0:T(8,128)}, u32[]{:S(2)}) copy-start(f32[16,512]{1,0:T(8,128)} %constant.36.clone.refs_3_) | copy-start | bytes 98308
  0.0 23.8 %copy-start.1 = (f32[2,512]{1,0:T(2,128)S(1)}, f32[2,512]{1,0:T(2,128)}, u32[]{:S(2)}) copy-start(f32[2,512]{1,0:T(2,128)} %constant.35.clone.refs_2_) | copy-start | bytes 12292
  0.0 13.7 %copy-start.2 = (s32[3,2]{0,1:T(2,128)S(1)}, s32[3,2]{0,1:T(2,128)}, u32[]{:S(2)}) copy-start(s32[3,2]{0,1:T(2,128)} %param.9) | copy-start | bytes 76
  8.0 12.4 %collective-permute-start = (bf16[3,128,1024]{2,1,0:T(8,128)(2,1)S(1)}, bf16[3,128,1024]{2,1,0:T(8,128)(2,1)S(1)}, u32[]{:S(2)}, u32[]{:S(2)}) collective-permute-start(bf16[3,128,1024]{2,1,0:T(8,128)(2,1)S(1)} %get-tuple-element.8.refs_4_.refs_8_.refs_9_.refs_7_), channel_id=1, source_target_pairs={{0,1},{1,0},{2,3},{3,2},{4,5},{5,4},{6,7},{7,6},{8,9},{9,8},{10,11... | collective-permute-start | bytes 2359304 | tf_op jit(solution)/shard_map/ppermute | solution.py:376
  8.1 15.7 %collective-permute-start.3 = (bf16[128,1024]{1,0:T(8,128)(2,1)S(1)}, bf16[128,1024]{1,0:T(8,128)(2,1)S(1)}, u32[]{:S(2)}, u32[]{:S(2)}) collective-permute-start(bf16[128,1024]{1,0:T(8,128)(2,1)S(1)} %get-tuple-element.9), channel_id=1, source_target_pairs={{2,0},{3,1},{4,2},{5,3},{6,4},{7,5},{8,6},{9,7},{10,8},{11,9},{12,... | collective-permute-start | bytes 786440 | tf_op jit(solution)/shard_map/ppermute | solution.py:374
  10.6 13.3 %collective-permute-start.4 = (bf16[128,1024]{1,0:T(8,128)(2,1)S(1)}, bf16[128,1024]{1,0:T(8,128)(2,1)S(1)}, u32[]{:S(2)}, u32[]{:S(2)}) collective-permute-start(bf16[128,1024]{1,0:T(8,128)(2,1)S(1)} %get-tuple-element.10), channel_id=1, source_target_pairs={{2,1},{4,3},{6,5},{8,7},{10,9},{12,11},{14,13},{18,17},{20,19},{22... | collective-permute-start | bytes 786440 | tf_op jit(solution)/shard_map/ppermute | solution.py:375
  13.7 5.5 %collective-permute-start.1 = (s32[3,2]{0,1:T(2,128)S(1)}, s32[3,2]{0,1:T(2,128)S(1)}, u32[]{:S(2)}, u32[]{:S(2)}) collective-permute-start(s32[3,2]{0,1:T(2,128)S(1)} %copy-done.2), channel_id=1, source_target_pairs={{0,2},{1,3},{2,4},{3,5},{4,6},{5,7},{6,8},{7,9},{8,10},{9,11},{10,... | collective-permute-start | bytes 80 | tf_op jit(solution)/shard_map/ppermute | solution.py:372
  20.5 12.4 %collective-permute-start.2 = (bf16[128,1024]{1,0:T(8,128)(2,1)S(1)}, bf16[128,1024]{1,0:T(8,128)(2,1)S(1)}, u32[]{:S(2)}, u32[]{:S(2)}) collective-permute-start(bf16[128,1024]{1,0:T(8,128)(2,1)S(1)} %select_bitcast_fusion), channel_id=1, source_target_pairs={{2,0},{3,1},{4,2},{5,3},{6,4},{7,5},{8,6},{9,7},{10,8},{11,9},{12,... | collective-permute-start | bytes 786440 | tf_op jit(solution)/shard_map/ppermute | solution.py:377
